TPU v7x, 128 devices: a whole 4x4x4 slice. The times are simulated.
128 devices in a mesh: grp: 2 (over core), seq: 64 (over y, x, z).
Axes of the slice: x: 4, y: 4, z: 4, core: 2. Of those that a mesh axis runs over, the one named last changes fastest.
Arguments:
- queries: bfloat16 [131072, 2048], P(('grp', 'seq')), may hold values from -6 to 6
- keys: bfloat16 [131072, 2048], P(('grp', 'seq')), may hold values from -6 to 6
- values: bfloat16 [131072, 2048], P(('grp', 'seq')), may hold values from -6 to 6
- log_decay: float32 [16, 131072], P(None, ('grp', 'seq')), may hold values from -1 to 0
- out_gate: bfloat16 [131072, 2048], P(('grp', 'seq')), may hold values from -6 to 6
- norm_gain: float32 [2048], replicated, may hold values from 0.25 to 1.75
Outputs:
- attended: bfloat16 [131072, 2048], P(('grp', 'seq'))
All inputs are finite; a program needn't handle non-finite values.
Results may differ from a plain program's by a relative error of at most 0.0052.
Values sent between devices are 32-bit elements; how exact they have to be, the bound alone decides.
No kernel may reach another device: no remote copies, remote signals or barrier semaphores. Data moves between devices by JAX's collectives and lax.ppermute only.
A program may use at most 320 MiB of HBM per device.

v0:
```python
import jax
import jax.numpy as jnp
from jax import lax
from jax.sharding import PartitionSpec as P


def entering(array, axis, combine, identity):
    count, place = (lax.axis_size(axis), lax.axis_index(axis))
    everything = jax.tree.map(lambda part: lax.all_gather(part, axis), array)
    start = jax.tree.map(
        lambda part, zero: jnp.broadcast_to(jnp.asarray(zero, part.dtype), part.shape),
        array,
        identity,
    )

    def lap(k, before):
        reached = k < place
        new = combine(before, jax.tree.map(lambda part: part[k], everything))
        return jax.tree.map(lambda a, b: jnp.where(reached, a, b), new, before)

    return lax.fori_loop(0, count, lap, start)


def from_root(block, axis, source):
    block = jnp.where(lax.axis_index(axis) == source, block, jnp.zeros_like(block))
    return lax.psum(block, axis)


def merge_states(earlier, later):
    return (earlier[0] + later[0], jnp.exp(later[0])[:, None, None] * earlier[1] + later[1])


def on_device(queries, keys, values, log_decay, out_gate, norm_gain):
    rows, feats = queries.shape
    heads = log_decay.shape[0]
    width = feats // heads
    q_three = queries.reshape(rows, heads, width)
    k_three = keys.reshape(rows, heads, width)
    v_three = values.reshape(rows, heads, width)
    cumul = jnp.cumsum(log_decay, axis=1)
    total = cumul[:, -1]
    scaled_keys = (
        k_three.astype(jnp.float32) * jnp.exp(total[None, :] - cumul.T)[:, :, None]
    ).astype(jnp.bfloat16)
    local_state = jnp.einsum(
        "thd,the->hde", scaled_keys, v_three, preferred_element_type=jnp.float32
    )
    own = (total, local_state)
    identity = (jnp.zeros((heads,), jnp.float32), jnp.zeros((heads, width, width), jnp.float32))
    inner = entering(own, "seq", merge_states, identity)
    inclusive_group = merge_states(inner, own)
    whole_group = (
        from_root(inclusive_group[0], "seq", lax.axis_size("seq") - 1),
        from_root(inclusive_group[1], "seq", lax.axis_size("seq") - 1),
    )
    carried = entering(whole_group, "grp", merge_states, identity)
    incoming = merge_states(carried, inner)[1]
    scores = jnp.einsum("thd,shd->hts", q_three, k_three, preferred_element_type=jnp.float32)
    gap = cumul[:, :, None] - cumul[:, None, :]
    occurrence_positions_list = jnp.arange(rows, dtype=jnp.int32)
    causal = occurrence_positions_list[:, None] >= occurrence_positions_list[None, :]
    weights = jnp.where(causal[None], jnp.exp(jnp.minimum(gap, 0.0)) * scores, 0.0).astype(
        jnp.bfloat16
    )
    intra = jnp.einsum("hts,shd->thd", weights, v_three, preferred_element_type=jnp.float32)
    rounded = incoming.astype(jnp.bfloat16)
    inter = jnp.einsum("thd,hde->the", q_three, rounded, preferred_element_type=jnp.float32)
    mixed = intra + jnp.exp(cumul).T[:, :, None] * inter
    power = jnp.mean(mixed * mixed, axis=-1, keepdims=True)
    normed = mixed * lax.rsqrt(power + 1e-06) * norm_gain.reshape(heads, width)
    gate = out_gate.reshape(rows, heads, width).astype(jnp.float32)
    return (normed * jax.nn.silu(gate)).astype(jnp.bfloat16).reshape(rows, feats)


def solution(mesh):
    in_specs = (
        P(("grp", "seq"), None),
        P(("grp", "seq"), None),
        P(("grp", "seq"), None),
        P(None, ("grp", "seq")),
        P(("grp", "seq"), None),
        P(),
    )
    out_specs = P(("grp", "seq"), None)
    return jax.shard_map(
        on_device, mesh=mesh, in_specs=in_specs, out_specs=out_specs, check_vma=False
    )
```

profile of v0, /device:TPU:1, one launch (start us, length us, event | category | flops | bytes accessed | tf_op | source)
XLA Modules:
  0.0 779.9 jit_solution(9645418334972572284)
XLA Ops:
  7.4 4.5 reduce-window.6
  12.6 6.4 copy.41
  19.0 5.9 fusion.7
  26.4 156.0 %all-reduce = f32[1024]{0:T(1024)S(1)} all-reduce(f32[1024]{0:T(1024)S(1)} %bitcast_dynamic-update-slice_fusion), channel_id=2, replica_groups=mesh['grp'=2,'seq'=64] {'seq'}, use_global_device_ids=true, to_apply=%add | all-reduce | flops 1024 | bytes 8192
  182.5 124.7 %all-gather.8.cloned.1.call-done = f32[1024,128,128]{2,1,0:T(8,128)} async-done(((f32[16,128,128]{2,1,0:T(8,128)}), f32[1024,128,128]{2,1,0:T(8,128)}) %all-gather.8.cloned.1.call-update) | async-done | bytes 67108880 | tf_op jit(solution)/shard_map/all_gather | solution.py:9
  307.2 96.5 %while.30 = (s32[]{:T(128)}, f32[16]{0:T(128)S(1)}, f32[16,128,128]{2,1,0:T(8,128)S(1)}, s32[]{:T(128)}, f32[64,16]{1,0:T(8,128)S(1)}, /*index=5*/f32[64,16,128,128]{3,2,1,0:T(8,128)}, s32[]{:T(128)}, s32[]{:T(128)}) while((s32[]{:T(128)}, f32[16]{0:T(128)S(1)}, f32[16,128,128]{2,1,0:T(8,128)S(1)}, s32[]{:T(128)}, ...), condition=%wide.region_3.4_spmd.clone, body=%wide.region_2.3_spmd.clone.sunk | while | flops 1048628 | bytes 3146163 | solution.py:21
  307.2 1.5 fusion.37
  308.8 1.5 fusion.37
  311.8 1.5 fusion.37
  313.4 1.5 fusion.37
  316.4 1.5 fusion.37
  319.4 1.5 fusion.37
  320.9 1.5 fusion.37
  322.4 1.5 fusion.37
  323.9 1.5 fusion.37
  326.9 1.5 fusion.37
  329.9 1.5 fusion.37
  331.4 1.5 fusion.37
  334.5 1.5 fusion.37
  337.5 1.5 fusion.37
  340.5 1.5 fusion.37
  342.0 1.5 fusion.37
  345.0 1.5 fusion.37
  348.0 1.5 fusion.37
  349.5 1.5 fusion.37
  351.0 1.5 fusion.37
  352.5 1.5 fusion.37
  355.6 1.5 fusion.37
  358.6 1.5 fusion.37
  360.1 1.5 fusion.37
  363.1 1.5 fusion.37
  366.1 1.5 fusion.37
  369.1 1.5 fusion.37
  370.6 1.5 fusion.37
  373.6 1.5 fusion.37
  376.7 1.5 fusion.37
  378.2 1.5 fusion.37
  379.7 1.5 fusion.37
  381.2 1.5 fusion.37
  405.0 126.9 %all-reduce.3.cloned.1.call-done = f32[1,16,128,128]{3,2,1,0:T(8,128)} async-done(((f32[1,16,128,128]{3,2,1,0:T(8,128)}), f32[1,16,128,128]{3,2,1,0:T(8,128)}) %all-reduce.3.cloned.1.call-update) | async-done | bytes 1048592 | tf_op jit(solution)/shard_map/psum | solution.py:26
  531.9 6.9 copy.37
  539.2 147.6 %psum.14 = f32[1,16]{1,0:T(1,128)S(1)} all-reduce(f32[1,16]{1,0:T(1,128)S(1)} %get-tuple-element.278), channel_id=1, replica_groups=mesh['grp'=2,'seq'=64] {'seq'}, use_global_device_ids=true, to_apply=%region_4.5 | all-reduce | flops 16 | bytes 128 | tf_op jit(solution)/shard_map/psum | solution.py:26
  686.8 31.6 %all-gather.2 = f32[2,1,16]{2,1,0:T(1,128)S(1)} all-gather(f32[1,1,16]{2,1,0:T(1,128)S(1)} %bitcast.107), channel_id=1, replica_groups=mesh['grp'=2,'seq'=64] {'grp'}, dimensions={0}, use_global_device_ids=true | all-gather | bytes 192 | tf_op jit(solution)/shard_map/all_gather | solution.py:9
  718.4 3.0 while.31
  721.4 7.5 fusion.10
  728.9 29.4 %multiply_reduce_fusion = (f32[1024,16]{0,1:T(8,128)S(1)}, f32[1024,16,128]{0,2,1:T(8,128)}) fusion(f32[16,128,1024]{2,1,0:T(8,128)} %fusion.10, f32[1024,16]{0,1:T(8,128)S(1)} %get-tuple-element.275, f32[16,1024]{1,0:T(8,128)S(1)} %bitcast.101, pred[1024,1024]{1,0:T(8,128)(4,1)S(1)} %iota_compare_fusion, bf16[1024,16,128]{0,2,1:T(8,128)(2,1)} %bitcast.96, ...), kind=kOutput, calls=%fused_computation.16 | convolution fusion | flops 8682192896 | bytes 30605312 | tf_op jit(solution)/shard_map/hts,shd->thd/dot_general | solution.py:65
  758.4 8.6 %multiply_convert_fusion = bf16[1024,16,128]{0,2,1:T(8,128)(2,1)} fusion(f32[1024,16,128]{0,2,1:T(8,128)} %bitcast.93, f32[1024,16,128]{0,2,1:T(8,128)} %get-tuple-element.281, f32[16,128]{1,0:T(8,128)S(1)} %bitcast.104, f32[1024,16]{0,1:T(8,128)S(1)} %add_rsqrt_fusion), kind=kLoop, calls=%fused_computation.15 | loop fusion | flops 16777216 | bytes 21045248 | tf_op jit(solution)/shard_map/convert_element_type | solution.py:72
  766.9 6.4 copy.38
  (134 shorter events, 53.4 us)
Async XLA Ops:
  6.5 300.7 %all-gather.8.cloned.1.call-start = ((), (), s32[]{:S(2)}) async-start(), calls=%async_computation.2 | async-start | bytes 68157440 | tf_op jit(solution)/shard_map/all_gather | solution.py:9
  19.0 6.0 copy-start.2
  24.9 507.0 %all-reduce.3.cloned.1.call-start = ((), (), s32[]{:S(2)}) async-start(), calls=%async_computation | async-start | bytes 2097152 | tf_op jit(solution)/shard_map/psum | solution.py:26
  307.2 96.6 %copy-start = (f32[16,128,128]{2,1,0:T(8,128)S(1)}, f32[16,128,128]{2,1,0:T(8,128)}, u32[]{:S(2)}) copy-start(f32[16,128,128]{2,1,0:T(8,128)} %fusion.7) | copy-start | bytes 3145732
  405.0 313.5 %all-gather.6.cloned.1.call-start = ((), (), s32[]{:S(2)}) async-start(), calls=%async_computation.1 | async-start | bytes 3145728 | tf_op jit(solution)/shard_map/all_gather | solution.py:9
  728.9 29.5 %copy-start.1 = (f32[2048]{0:T(1024)S(1)}, f32[2048]{0:T(1024)}, u32[]{:S(2)}) copy-start(f32[2048]{0:T(1024)} %param.15) | copy-start | bytes 24580
Sparse Core Ops, SparseCore 0:
  25.0 282.1 all-gather.7
  405.1 126.7 all-reduce.2
  533.6 13.1 all-gather.5
where the time goes:
time: 783 us; the launch traced here: 780 us
  blocking collectives  335 us (43%)
  waiting for transfers between devices  252 us (32%)
  other arithmetic  112 us (14%)
  matrix products  42.8 us (5%)
  local copies, waits for them, and re-layouts  21.9 us (3%)
  between operations  13.9 us (2%)
    unnamed x1, blocking collectives  156 us
    psum x1, blocking collectives, from_root(): return lax.psum(block, axis)  148 us
    psum x1, waiting for transfers between devices, from_root(): return lax.psum(block, axis)  127 us
    all_gather x2, waiting for transfers between devices, entering(): everything = jax.tree.map(lambda part: lax.all_gather(part, axis), array)  125 us
    select_n x66, other arithmetic, lap(): return jax.tree.map(lambda a, b: jnp.where(reached, a, b), new, before)  96.5 us
    all_gather x1, blocking collectives, entering(): everything = jax.tree.map(lambda part: lax.all_gather(part, axis), array)  31.6 us
    dot_general x1, matrix products, on_device(): jnp.einsum('hts,shd->thd', weights, v_three, preferred_element_type=jnp.f...  29.4 us
  transfers between devices with their start and end apart: 3, of which 2 were waited for; matrix products, arithmetic and copies ran while one was open for 1% of the time, Pallas kernels for 0%

commit v1 on v0

v1 whole, which is shorter than its diff:
```python
import functools

import jax
import jax.numpy as jnp
from jax import lax
from jax.experimental import pallas as pl
from jax.experimental.pallas import tpu as pltpu
from jax.sharding import PartitionSpec as P

AXES = ("grp", "seq")
MIB = 1 << 20
LOW = -1e30


def running_sum(decay):
    heads, rows = decay.shape
    a = lax.broadcasted_iota(jnp.int32, (128, 128), 0)
    b = lax.broadcasted_iota(jnp.int32, (128, 128), 1)
    upper = (a <= b).astype(jnp.float32)
    carry = jnp.zeros((heads, 1), jnp.float32)
    parts = []
    for c in range(rows // 128):
        part = jnp.dot(
            decay[:, c * 128 : (c + 1) * 128],
            upper,
            precision=lax.Precision.HIGHEST,
            preferred_element_type=jnp.float32,
        )
        part = part + carry
        carry = part[:, 127:128]
        parts.append(part)
    return jnp.concatenate(parts, axis=1)


def across(first, second):
    zero = jnp.zeros_like(first)
    return jnp.concatenate(
        [jnp.concatenate([first, zero], axis=1), jnp.concatenate([zero, second], axis=1)], axis=0
    )


def state_kernel(group, width, piece, tile, decay_ref, k_ref, v_ref, send_ref, near_ref, cumul_ref, sum_ref):
    step = pl.program_id(0)
    rows = k_ref.shape[0]

    @pl.when(step == 0)
    def _():
        cumul = running_sum(decay_ref[...])
        sum_ref[...] = cumul
        cumul_ref[...] = cumul

    per = width // piece
    parts = rows // tile
    for i in range(group):
        row = sum_ref[pl.ds(step * group + i, 1), :]
        cut = slice(i * width, (i + 1) * width)
        before = jnp.zeros((1, 1), jnp.float32)
        state = None
        for t in range(parts):
            mine = slice(t * tile, (t + 1) * tile)
            total = row[:, (t + 1) * tile - 1 : (t + 1) * tile]
            scale = jnp.exp(total - row[:, mine])
            keys = k_ref[mine, cut].T.astype(jnp.float32)
            scaled = (keys * scale).astype(jnp.bfloat16)
            fresh = jnp.dot(scaled, v_ref[mine, cut], preferred_element_type=jnp.float32)
            state = fresh if t == 0 else state * jnp.exp(total - before) + fresh
            before = total
            if t < parts - 1:
                at = (i * (parts - 1) + t) * width
                near_ref[at : at + width, :] = state.astype(jnp.bfloat16)
        factor = jnp.broadcast_to(jnp.exp(total), (8, width))
        for p in range(per):
            send_ref[i * per + p, 0:piece, :] = state[p * piece : (p + 1) * piece, :]
            send_ref[i * per + p, piece : piece + 8, :] = factor


def scan_kernel(piece, got_ref, out_ref):
    count = got_ref.shape[0]
    width = got_ref.shape[2]

    def lap(j, carry):
        out_ref[j, :, :] = carry
        factor = got_ref[j, piece : piece + 1, :]
        return carry * factor + got_ref[j, 0:piece, :]

    lax.fori_loop(0, count, lap, jnp.zeros((piece, width), jnp.float32), unroll=8)


def intra_kernel(group, width, tile, cumul_ref, near_ref, q_ref, k_ref, v_ref, out_ref):
    step = pl.program_id(0)
    rows = q_ref.shape[0]
    parts = rows // tile
    a = lax.broadcasted_iota(jnp.int32, (tile, tile), 0)
    b = lax.broadcasted_iota(jnp.int32, (tile, tile), 1)
    mask = jnp.where(a >= b, 0.0, LOW)
    for i in range(0, group, 2):
        row = [cumul_ref[pl.ds(step * group + i + n, 1), :] for n in range(2)]
        col = [jnp.broadcast_to(r, (8, rows)).T[:, 0:1] for r in row]
        both = slice(i * width, (i + 2) * width)
        for t in range(parts):
            start = t * tile
            mine = slice(start, start + tile)
            if t:
                at = [((i + n) * (parts - 1) + t - 1) * width for n in range(2)]
                far = jnp.dot(
                    q_ref[mine, both],
                    across(*(near_ref[x : x + width, :] for x in at)),
                    preferred_element_type=jnp.float32,
                )
            for n in range(2):
                cut = slice((i + n) * width, (i + n + 1) * width)
                scores = lax.dot_general(
                    q_ref[mine, cut],
                    k_ref[mine, cut],
                    (((1,), (1,)), ((), ())),
                    preferred_element_type=jnp.float32,
                )
                gap = col[n][mine] - row[n][:, mine] + mask
                weights = (jnp.exp(gap) * scores).astype(jnp.bfloat16)
                intra = jnp.dot(weights, v_ref[mine, cut], preferred_element_type=jnp.float32)
                if t:
                    edge = row[n][:, start - 1 : start]
                    intra = intra + jnp.exp(col[n][mine] - edge) * far[:, n * width : (n + 1) * width]
                out_ref[mine, cut] = intra.astype(out_ref.dtype)


def ready_kernel(group, width, cumul_ref, q_ref, gate_ref, gain_ref, scaled_ref, gated_ref):
    step = pl.program_id(0)
    rows = q_ref.shape[0]
    gate = gate_ref[...].astype(jnp.float32)
    gated = gain_ref[...] * (gate / (1.0 + jnp.exp(-gate)))
    gated_ref[...] = gated.astype(gated_ref.dtype)
    for i in range(group):
        cut = slice(i * width, (i + 1) * width)
        row = jnp.exp(cumul_ref[pl.ds(step * group + i, 1), :])
        col = jnp.broadcast_to(row, (8, rows)).T[:, 0:1]
        scaled_ref[:, cut] = (q_ref[:, cut].astype(jnp.float32) * col).astype(jnp.bfloat16)


def final_kernel(group, width, state_ref, q_ref, intra_ref, gated_ref, out_ref):
    share = jnp.full((width, width), 1.0 / width, jnp.bfloat16)
    share = across(share, share)
    for i in range(0, group, 2):
        both = slice(i * width, (i + 2) * width)
        state = state_ref[i * width : (i + 2) * width, :].astype(jnp.bfloat16)
        mixed = intra_ref[:, both].astype(jnp.float32) + jnp.dot(
            q_ref[:, both],
            across(state[0:width], state[width:]),
            preferred_element_type=jnp.float32,
        )
        power = jnp.dot(
            (mixed * mixed).astype(jnp.bfloat16), share, preferred_element_type=jnp.float32
        )
        out = mixed * lax.rsqrt(power + 1e-6) * gated_ref[:, both].astype(jnp.float32)
        out_ref[:, both] = out.astype(jnp.bfloat16)


def on_device(count, queries, keys, values, log_decay, out_gate, norm_gain):
    rows, feats = queries.shape
    heads = log_decay.shape[0]
    width = feats // heads
    piece = heads * width // count
    tile = 256
    parts = rows // tile
    f32, bf16 = jnp.float32, jnp.bfloat16

    def whole(*shape):
        return pl.BlockSpec(shape, lambda s: (0,) * len(shape))

    def cols(group):
        return pl.BlockSpec((rows, group * width), lambda s: (0, s))

    def lines(n):
        return pl.BlockSpec((n, width), lambda s: (s, 0))

    def gain(group):
        return pl.BlockSpec((1, group * width), lambda s: (0, s))

    def like(dtype):
        return jax.ShapeDtypeStruct((rows, feats), dtype)

    def call(name, body, group, ins, outs, shapes, flops, moved, exps, scratch=()):
        return pl.pallas_call(
            body,
            grid=(heads // group,),
            in_specs=ins,
            out_specs=outs,
            out_shape=shapes,
            scratch_shapes=list(scratch),
            compiler_params=pltpu.CompilerParams(vmem_limit_bytes=60 * MIB),
            cost_estimate=pl.CostEstimate(flops=flops, bytes_accessed=moved, transcendentals=exps),
            name=name,
        )

    group = 4
    send, near, cumul = call(
        "states",
        functools.partial(state_kernel, group, width, piece, tile),
        group,
        [whole(heads, rows), cols(group), cols(group)],
        [
            pl.BlockSpec((group * width // piece, piece + 8, width), lambda s: (s, 0, 0)),
            lines(group * (parts - 1) * width),
            whole(heads, rows),
        ],
        [
            jax.ShapeDtypeStruct((count, piece + 8, width), f32),
            jax.ShapeDtypeStruct((heads * (parts - 1) * width, width), bf16),
            jax.ShapeDtypeStruct((heads, rows), f32),
        ],
        2 * rows * feats * width,
        12 * MIB,
        heads * rows,
        [pltpu.VMEM((heads, rows), f32)],
    )(log_decay, keys, values)
    got = lax.all_to_all(send, AXES, 0, 0, tiled=True)
    group = 2
    intra = call(
        "intra",
        functools.partial(intra_kernel, group, width, tile),
        group,
        [whole(heads, rows), lines(group * (parts - 1) * width), *[cols(group)] * 3],
        cols(group),
        like(bf16),
        4 * rows * tile * feats,
        18 * MIB,
        heads * rows * tile,
    )(cumul, near, queries, keys, values)
    got, intra = lax.optimization_barrier((got, intra))
    entering = pl.pallas_call(
        functools.partial(scan_kernel, piece),
        out_shape=jax.ShapeDtypeStruct((count, piece, width), f32),
        compiler_params=pltpu.CompilerParams(vmem_limit_bytes=8 * MIB),
        cost_estimate=pl.CostEstimate(
            flops=2 * heads * width * width, bytes_accessed=3 * MIB, transcendentals=0
        ),
        name="scan",
    )(got)
    incoming = lax.all_to_all(entering, AXES, 0, 0, tiled=True).reshape(heads * width, width)
    group = 4
    scaled, gated = call(
        "ready",
        functools.partial(ready_kernel, group, width),
        group,
        [whole(heads, rows), cols(group), cols(group), gain(group)],
        [cols(group), cols(group)],
        [like(bf16), like(bf16)],
        40 * rows * feats,
        16 * MIB,
        2 * rows * feats,
    )(cumul, queries, out_gate, norm_gain.reshape(1, feats))
    incoming, scaled, gated = lax.optimization_barrier((incoming, scaled, gated))
    return call(
        "final",
        functools.partial(final_kernel, group, width),
        group,
        [lines(group * width), *[cols(group)] * 3],
        cols(group),
        like(bf16),
        4 * rows * feats * width,
        17 * MIB,
        rows * feats,
    )(incoming, scaled, intra, gated)


def solution(mesh):
    split = P(AXES, None)
    count = 1
    for axis in AXES:
        count *= mesh.shape[axis]
    return jax.shard_map(
        functools.partial(on_device, count),
        mesh=mesh,
        in_specs=(split, split, split, P(None, AXES), split, P()),
        out_specs=split,
        check_vma=False,
    )
```

time: 783 us -> 77.3 us (0.10)
  blocking collectives: 335 us -> 0 us
  waiting for transfers between devices: 252 us -> 13.5 us
  other arithmetic: 112 us -> 0 us
  Pallas kernels: 0 us -> 44.6 us
  matrix products: 42.8 us -> 0 us
  local copies, waits for them, and re-layouts: 21.9 us -> 1.04 us
  starting transfers between devices: 0.09 us -> 17.7 us
  between operations: 13.9 us -> 0.02 us
    unnamed x1 -> x0, blocking collectives: 156 us -> none
    psum x1 -> x0, blocking collectives: 148 us -> none  [from_root(): return lax.psum(block, axis)]
    psum x1 -> x0, waiting for transfers between devices: 127 us -> none  [from_root(): return lax.psum(block, axis)]
    all_gather x2 -> x0, waiting for transfers between devices: 125 us -> none  [entering(): everything = jax.tree.map(lambda part: lax.all_gather(part, axis), array)]
    select_n x66 -> x0, other arithmetic: 96.5 us -> none  [lap(): return jax.tree.map(lambda a, b: jnp.where(reached, a, b), new, before)]
    pallas_call x0 -> x5, Pallas kernels: none -> 44.6 us  [the longest x1 15.4 us: on_device(): call('intra', functools.partial(intra_kernel, group, width, tile), group,...]
    dot_general x3 -> x0, matrix products: 42.8 us -> none  [the longest x1 29.4 us: on_device(): jnp.einsum('hts,shd->thd', weights, v_three, preferred_element_type=jnp.f...]
    all_gather x1 -> x0, blocking collectives: 31.6 us -> none  [entering(): everything = jax.tree.map(lambda part: lax.all_gather(part, axis), array)]
  transfers between devices with their start and end apart: 3 -> 2, of which waited for: 2 -> 2; matrix products, arithmetic and copies ran while one was open for 1% -> 0% of each run, Pallas kernels for 0% -> 35%
where the time goes in v1:
time: 77.3 us; the launch traced here: 76.9 us
  Pallas kernels  44.6 us (58%)
  starting transfers between devices  17.7 us (23%)
  waiting for transfers between devices  13.5 us (17%)
  local copies, waits for them, and re-layouts  1.04 us (1%)
    pallas_call x1, Pallas kernels, on_device(): call('intra', functools.partial(intra_kernel, group, width, tile), group,...  15.4 us
    pallas_call x1, Pallas kernels, on_device(): call('ready', functools.partial(ready_kernel, group, width), group, [whol...  11.7 us
    all_to_all x1, starting transfers between devices, on_device(): got = lax.all_to_all(send, AXES, 0, 0, tiled=True)  11.5 us
    pallas_call x1, Pallas kernels, on_device(): call('final', functools.partial(final_kernel, group, width), group, [line...  8.57 us
    pallas_call x1, Pallas kernels, on_device(): call('states', functools.partial(state_kernel, group, width, piece, tile)...  7.61 us
    all_to_all x1, waiting for transfers between devices, on_device(): got = lax.all_to_all(send, AXES, 0, 0, tiled=True)  7.57 us
    all_to_all x1, starting transfers between devices, on_device(): lax.all_to_all(entering, AXES, 0, 0, tiled=True)  6.2 us
    all_to_all x1, waiting for transfers between devices, on_device(): lax.all_to_all(entering, AXES, 0, 0, tiled=True)  5.93 us
  transfers between devices with their start and end apart: 2, of which 2 were waited for; matrix products, arithmetic and copies ran while one was open for 0% of the time, Pallas kernels for 35%

profile of v1, /device:TPU:1, one launch (start us, length us, event | category | flops | bytes accessed | tf_op | source)
XLA Modules:
  0.0 76.9 jit_solution(2383115776371571408)
XLA Ops:
  0.0 7.6 %states.1 = (f32[128,24,128]{2,1,0:T(8,128)}, bf16[6144,128]{1,0:T(8,128)(2,1)}, f32[16,1024]{1,0:T(8,128)}) custom-call(f32[16,1024]{1,0:T(8,128)} %decay_ref.1, bf16[1024,2048]{1,0:T(8,128)(2,1)} %k_ref.3, bf16[1024,2048]{1,0:T(8,128)(2,1)} %v_ref.3), custom_call_target="tpu_custom_call" | custom-call | flops 536870912 | bytes 12582912 | tf_op jit(solution)/shard_map/states/pallas_call | solution.py:196
  7.6 11.5 %all-to-all-start = ((f32[128,24,128]{2,1,0:T(8,128)}), f32[128,24,128]{2,1,0:T(8,128)S(1)}, u32[]{:S(2)}, u32[]{:S(2)}) async-start(f32[128,24,128]{2,1,0:T(8,128)} %get-tuple-element.15), calls=%async_computation | async-start | bytes 3145728 | tf_op jit(solution)/shard_map/all_to_all | solution.py:216
  19.1 15.4 %intra.1.intra_ref = bf16[1024,2048]{1,0:T(8,128)(2,1)} custom-call(f32[16,1024]{1,0:T(8,128)} %get-tuple-element.16.cumul_ref, bf16[6144,128]{1,0:T(8,128)(2,1)} %get-tuple-element.17.near_ref, bf16[1024,2048]{1,0:T(8,128)(2,1)} %q_ref.3, bf16[1024,2048]{1,0:T(8,128)(2,1)} %k_ref.3, bf16[1024,2048]{1,0:T(8,128)(2,1)} %v_ref.3), custom_call_target="tpu_custom_call" | custom-call | flops 2147483648 | bytes 18874368 | tf_op jit(solution)/shard_map/intra/pallas_call | solution.py:218
  34.6 7.6 %all-to-all-done.got_ref = f32[128,24,128]{2,1,0:T(8,128)S(1)} async-done(((f32[128,24,128]{2,1,0:T(8,128)}), f32[128,24,128]{2,1,0:T(8,128)S(1)}, u32[]{:S(2)}, u32[]{:S(2)}) %all-to-all-start) | async-done | bytes 1572896 | tf_op jit(solution)/shard_map/all_to_all | solution.py:216
  42.1 1.3 %scan.1 = f32[128,16,128]{2,1,0:T(8,128)} custom-call(f32[128,24,128]{2,1,0:T(8,128)S(1)} %all-to-all-done.got_ref), custom_call_target="tpu_custom_call" | custom-call | flops 524288 | bytes 3145728 | tf_op jit(solution)/shard_map/scan/pallas_call | solution.py:230
  43.4 6.2 %all-to-all-start.1 = ((f32[128,16,128]{2,1,0:T(8,128)}), f32[128,16,128]{2,1,0:T(8,128)S(1)}, u32[]{:S(2)}, u32[]{:S(2)}) async-start(f32[128,16,128]{2,1,0:T(8,128)} %scan.1), calls=%async_computation.1 | async-start | bytes 2097152 | tf_op jit(solution)/shard_map/all_to_all | solution.py:239
  49.6 11.7 %ready.1 = (bf16[1024,2048]{1,0:T(8,128)(2,1)}, bf16[1024,2048]{1,0:T(8,128)(2,1)}) custom-call(f32[16,1024]{1,0:T(8,128)} %get-tuple-element.16.cumul_ref, bf16[1024,2048]{1,0:T(8,128)(2,1)} %q_ref.3, bf16[1024,2048]{1,0:T(8,128)(2,1)} %gate_ref.1, f32[1,2048]{1,0:T(1,128)} %bitcast.3), custom_call_target="tpu_custom_call" | custom-call | flops 83886080 | bytes 16777216 | tf_op jit(solution)/shard_map/ready/pallas_call | solution.py:241
  61.3 5.9 %all-to-all-done.1 = f32[128,16,128]{2,1,0:T(8,128)S(1)} async-done(((f32[128,16,128]{2,1,0:T(8,128)}), f32[128,16,128]{2,1,0:T(8,128)S(1)}, u32[]{:S(2)}, u32[]{:S(2)}) %all-to-all-start.1) | async-done | bytes 1048608 | tf_op jit(solution)/shard_map/all_to_all | solution.py:239
  67.2 0.0 copy-start
  67.2 1.0 %copy-done = f32[128,16,128]{2,1,0:T(8,128)} copy-done((f32[128,16,128]{2,1,0:T(8,128)}, f32[128,16,128]{2,1,0:T(8,128)S(1)}, u32[]{:S(2)}) %copy-start) | copy-done | bytes 1048600
  68.3 8.6 %final.1 = bf16[1024,2048]{1,0:T(8,128)(2,1)} custom-call(f32[2048,128]{1,0:T(8,128)} %bitcast.2, bf16[1024,2048]{1,0:T(8,128)(2,1)} %get-tuple-element.22.q_ref, bf16[1024,2048]{1,0:T(8,128)(2,1)} %intra.1.intra_ref, bf16[1024,2048]{1,0:T(8,128)(2,1)} %get-tuple-element.24.gated_ref), custom_call_target="tpu_custom_call" | custom-call | flops 1073741824 | bytes 17825792 | tf_op jit(solution)/shard_map/final/pallas_call | solution.py:253
Async XLA Ops:
  7.6 34.5 %all-to-all-start = ((f32[128,24,128]{2,1,0:T(8,128)}), f32[128,24,128]{2,1,0:T(8,128)S(1)}, u32[]{:S(2)}, u32[]{:S(2)}) async-start(f32[128,24,128]{2,1,0:T(8,128)} %get-tuple-element.15), calls=%async_computation | async-start | bytes 3145728 | tf_op jit(solution)/shard_map/all_to_all | solution.py:216
  43.4 23.9 %all-to-all-start.1 = ((f32[128,16,128]{2,1,0:T(8,128)}), f32[128,16,128]{2,1,0:T(8,128)S(1)}, u32[]{:S(2)}, u32[]{:S(2)}) async-start(f32[128,16,128]{2,1,0:T(8,128)} %scan.1), calls=%async_computation.1 | async-start | bytes 2097152 | tf_op jit(solution)/shard_map/all_to_all | solution.py:239
  67.2 1.0 %copy-start = (f32[128,16,128]{2,1,0:T(8,128)}, f32[128,16,128]{2,1,0:T(8,128)S(1)}, u32[]{:S(2)}) copy-start(f32[128,16,128]{2,1,0:T(8,128)S(1)} %all-to-all-done.1) | copy-start | bytes 3145732

commit v2 on v1

v2 whole, which is shorter than its diff:
```python
import functools

import jax
import jax.numpy as jnp
from jax import lax
from jax.experimental import pallas as pl
from jax.experimental.pallas import tpu as pltpu
from jax.sharding import PartitionSpec as P

AXES = ("grp", "seq")
MIB = 1 << 20
LOW = -1e30


def running_sum(decay):
    heads, rows = decay.shape
    a = lax.broadcasted_iota(jnp.int32, (128, 128), 0)
    b = lax.broadcasted_iota(jnp.int32, (128, 128), 1)
    upper = (a <= b).astype(jnp.float32)
    carry = jnp.zeros((heads, 1), jnp.float32)
    parts = []
    for c in range(rows // 128):
        part = jnp.dot(
            decay[:, c * 128 : (c + 1) * 128],
            upper,
            precision=lax.Precision.HIGHEST,
            preferred_element_type=jnp.float32,
        )
        part = part + carry
        carry = part[:, 127:128]
        parts.append(part)
    return jnp.concatenate(parts, axis=1)


def across(first, second):
    zero = jnp.zeros_like(first)
    return jnp.concatenate(
        [jnp.concatenate([first, zero], axis=1), jnp.concatenate([zero, second], axis=1)], axis=0
    )


def fetch(source, target, sems, chunks):
    wide = source.shape[1] // chunks
    return [
        pltpu.make_async_copy(
            source.at[:, pl.ds(c * wide, wide)], target.at[:, pl.ds(c * wide, wide)], sems.at[c]
        )
        for c in range(chunks)
    ]


def state_kernel(
    width, piece, tile, chunks, decay_ref, k_far, v_far, send_far, near_far, cumul_far, k_ref, v_ref,
    stage_ref, near_ref, cumul_ref, k_sems, v_sems, sems, near_sems, cumul_sem,
):
    rows, feats = k_ref.shape
    heads = feats // width
    copies = list(zip(fetch(k_far, k_ref, k_sems, chunks), fetch(v_far, v_ref, v_sems, chunks)))
    ahead = 4
    for pair in copies[:ahead]:
        for copy in pair:
            copy.start()
    cumul = running_sum(decay_ref[...])
    cumul_ref[...] = cumul
    cumul_copy = pltpu.make_async_copy(cumul_ref, cumul_far, cumul_sem)
    cumul_copy.start()

    group = heads // chunks
    per = width // piece
    pairs = piece // 2 + 1
    parts = rows // tile
    sent = []
    for c in range(chunks):
        for copy in copies[c]:
            copy.wait()
        if c + ahead < chunks:
            for copy in copies[c + ahead]:
                copy.start()
        for i in range(c * group, (c + 1) * group):
            row = cumul[i : i + 1, :]
            cut = slice(i * width, (i + 1) * width)
            before = jnp.zeros((1, 1), jnp.float32)
            state = None
            for t in range(parts):
                mine = slice(t * tile, (t + 1) * tile)
                total = row[:, (t + 1) * tile - 1 : (t + 1) * tile]
                scale = jnp.exp(total - row[:, mine])
                keys = k_ref[mine, cut].T.astype(jnp.float32)
                scaled = (keys * scale).astype(jnp.bfloat16)
                fresh = jnp.dot(scaled, v_ref[mine, cut], preferred_element_type=jnp.float32)
                state = fresh if t == 0 else state * jnp.exp(total - before) + fresh
                before = total
                if t < parts - 1:
                    at = (i * (parts - 1) + t) * width
                    near_ref[at : at + width, :] = state.astype(jnp.bfloat16)
            factor = jnp.broadcast_to(jnp.exp(total), (2, width))
            for p in range(per):
                at = (i * per + p) * pairs
                for r in range(pairs - 1):
                    from_row = p * piece + 2 * r
                    stage_ref[at + r, :, :] = state[from_row : from_row + 2, :]
                stage_ref[at + pairs - 1, :, :] = factor
        for held, far, sem, each in (
            (stage_ref, send_far, sems, group * per * pairs),
            (near_ref, near_far, near_sems, group * (parts - 1) * width),
        ):
            some = pl.ds(c * each, each)
            copy = pltpu.make_async_copy(held.at[some], far.at[some], sem.at[c])
            copy.start()
            sent.append(copy)
    cumul_copy.wait()
    for copy in sent:
        copy.wait()


def scan_kernel(pairs, got_ref, out_ref):
    count = out_ref.shape[0]
    width = got_ref.shape[2]

    def lap(j, carry):
        at = j * pairs
        factor = got_ref[at + pairs - 1]
        for r in range(pairs - 1):
            out_ref[j, 2 * r : 2 * r + 2, :] = carry[r]
        return tuple(carry[r] * factor + got_ref[at + r] for r in range(pairs - 1))

    zero = jnp.zeros((2, width), jnp.float32)
    lax.fori_loop(0, count, lap, (zero,) * (pairs - 1), unroll=8)


def intra_kernel(
    width, tile, chunks, cumul_ref, near_ref, q_far, k_far, v_far, out_far, q_ref, k_ref, v_ref,
    out_ref, q_sems, k_sems, v_sems, sems,
):
    rows, feats = q_ref.shape
    heads = feats // width
    group = heads // chunks
    copies = list(
        zip(
            fetch(q_far, q_ref, q_sems, chunks),
            fetch(k_far, k_ref, k_sems, chunks),
            fetch(v_far, v_ref, v_sems, chunks),
        )
    )
    sent = fetch(out_ref, out_far, sems, chunks)
    for some in copies:
        for copy in some:
            copy.start()
    parts = rows // tile
    a = lax.broadcasted_iota(jnp.int32, (tile, tile), 0)
    b = lax.broadcasted_iota(jnp.int32, (tile, tile), 1)
    mask = jnp.where(a >= b, 0.0, LOW)
    columns = jnp.concatenate(
        [cumul_ref[...], jnp.zeros((width - heads, rows), jnp.float32)], axis=0
    ).T
    for i in range(0, heads, 2):
        if i % group == 0:
            for copy in copies[i // group]:
                copy.wait()
        row = [cumul_ref[i + n : i + n + 1, :] for n in range(2)]
        col = [columns[:, i + n : i + n + 1] for n in range(2)]
        both = slice(i * width, (i + 2) * width)
        for t in range(parts):
            start = t * tile
            mine = slice(start, start + tile)
            if t:
                at = [((i + n) * (parts - 1) + t - 1) * width for n in range(2)]
                far = jnp.dot(
                    q_ref[mine, both],
                    across(*(near_ref[x : x + width, :] for x in at)),
                    preferred_element_type=jnp.float32,
                )
            for n in range(2):
                cut = slice((i + n) * width, (i + n + 1) * width)
                scores = lax.dot_general(
                    q_ref[mine, cut],
                    k_ref[mine, cut],
                    (((1,), (1,)), ((), ())),
                    preferred_element_type=jnp.float32,
                )
                gap = col[n][mine] - row[n][:, mine] + mask
                weights = (jnp.exp(gap) * scores).astype(jnp.bfloat16)
                intra = jnp.dot(weights, v_ref[mine, cut], preferred_element_type=jnp.float32)
                if t:
                    edge = row[n][:, start - 1 : start]
                    intra = intra + jnp.exp(col[n][mine] - edge) * far[:, n * width : (n + 1) * width]
                out_ref[mine, cut] = intra.astype(out_ref.dtype)
        if (i + 2) % group == 0:
            sent[i // group].start()
    for copy in sent:
        copy.wait()


def ready_kernel(
    width, chunks, cumul_ref, q_far, gate_far, gain_ref, scaled_far, gated_far, q_ref, gate_ref,
    scaled_ref, gated_ref, q_sems, gate_sems, scaled_sems, gated_sems,
):
    rows, feats = q_ref.shape
    heads = feats // width
    gates = fetch(gate_far, gate_ref, gate_sems, chunks)
    queries = fetch(q_far, q_ref, q_sems, chunks)
    sent = list(
        zip(
            fetch(scaled_ref, scaled_far, scaled_sems, chunks),
            fetch(gated_ref, gated_far, gated_sems, chunks),
        )
    )
    group = heads // chunks
    for c in range(chunks):
        gates[c].start()
        queries[c].start()
    columns = jnp.concatenate(
        [jnp.exp(cumul_ref[...]), jnp.zeros((width - heads, rows), jnp.float32)], axis=0
    ).T
    for i in range(heads):
        if i % group == 0:
            gates[i // group].wait()
            queries[i // group].wait()
        cut = slice(i * width, (i + 1) * width)
        half = gate_ref[:, cut].astype(jnp.float32) * 0.5
        gated_ref[:, cut] = (gain_ref[:, cut] * (half + half * jnp.tanh(half))).astype(gated_ref.dtype)
        scaled = q_ref[:, cut].astype(jnp.float32) * columns[:, i : i + 1]
        scaled_ref[:, cut] = scaled.astype(scaled_ref.dtype)
        if (i + 1) % group == 0:
            for copy in sent[i // group]:
                copy.start()
    for some in sent:
        for copy in some:
            copy.wait()


def final_kernel(
    width, tile, chunks, state_ref, q_far, intra_far, gated_far, out_far, q_ref, intra_ref, gated_ref,
    out_ref, q_sems, intra_sems, gated_sems, sems,
):
    rows, feats = q_ref.shape
    heads = feats // width
    group = heads // chunks
    copies = list(
        zip(
            fetch(q_far, q_ref, q_sems, chunks),
            fetch(intra_far, intra_ref, intra_sems, chunks),
            fetch(gated_far, gated_ref, gated_sems, chunks),
        )
    )
    sent = fetch(out_ref, out_far, sems, chunks)
    for some in copies:
        for copy in some:
            copy.start()
    share = jnp.full((width, width), 1.0 / width, jnp.bfloat16)
    share = across(share, share)
    for i in range(0, heads, 2):
        if i % group == 0:
            for copy in copies[i // group]:
                copy.wait()
        both = slice(i * width, (i + 2) * width)
        state = state_ref[i * width : (i + 2) * width, :].astype(jnp.bfloat16)
        state = across(state[0:width], state[width:])
        for t in range(rows // tile):
            mine = slice(t * tile, (t + 1) * tile)
            mixed = intra_ref[mine, both].astype(jnp.float32) + jnp.dot(
                q_ref[mine, both], state, preferred_element_type=jnp.float32
            )
            power = jnp.dot(
                (mixed * mixed).astype(jnp.bfloat16), share, preferred_element_type=jnp.float32
            )
            out = mixed * lax.rsqrt(power + 1e-6) * gated_ref[mine, both].astype(jnp.float32)
            out_ref[mine, both] = out.astype(jnp.bfloat16)
        if (i + 2) % group == 0:
            sent[i // group].start()
    for copy in sent:
        copy.wait()


def on_device(count, queries, keys, values, log_decay, out_gate, norm_gain):
    rows, feats = queries.shape
    heads = log_decay.shape[0]
    width = feats // heads
    piece = heads * width // count
    tile = 256
    parts = rows // tile
    chunks = 8
    f32, bf16 = jnp.float32, jnp.bfloat16
    here = pl.BlockSpec(memory_space=pltpu.VMEM)
    there = pl.BlockSpec(memory_space=pl.ANY)
    block = (rows, feats)
    sems = pltpu.SemaphoreType.DMA((chunks,))
    held = pltpu.VMEM(block, bf16)
    moved = jax.ShapeDtypeStruct(block, bf16)

    def call(name, body, ins, outs, shapes, flops, bytes_moved, exps, limit, scratch=()):
        return pl.pallas_call(
            body,
            in_specs=ins,
            out_specs=outs,
            out_shape=shapes,
            scratch_shapes=list(scratch),
            compiler_params=pltpu.CompilerParams(vmem_limit_bytes=limit * MIB),
            cost_estimate=pl.CostEstimate(flops=flops, bytes_accessed=bytes_moved, transcendentals=exps),
            name=name,
        )

    pairs = piece // 2 + 1
    message = (count * pairs, 2, width)
    inner = (heads * (parts - 1) * width, width)
    send, near, cumul = call(
        "states",
        functools.partial(state_kernel, width, piece, tile, chunks),
        [here, there, there],
        [there, there, there],
        [
            jax.ShapeDtypeStruct(message, f32),
            jax.ShapeDtypeStruct(inner, bf16),
            jax.ShapeDtypeStruct((heads, rows), f32),
        ],
        2 * rows * feats * width,
        12 * MIB,
        heads * rows,
        56,
        [
            held,
            held,
            pltpu.VMEM(message, f32),
            pltpu.VMEM(inner, bf16),
            pltpu.VMEM((heads, rows), f32),
            *[sems] * 4,
            pltpu.SemaphoreType.DMA,
        ],
    )(log_decay, keys, values)
    got = lax.all_to_all(send, AXES, 0, 0, tiled=True)
    intra = call(
        "intra",
        functools.partial(intra_kernel, width, tile, chunks),
        [here, here, there, there, there],
        there,
        moved,
        4 * rows * tile * feats,
        18 * MIB,
        heads * rows * tile,
        56,
        [*[held] * 4, *[sems] * 4],
    )(cumul, near, queries, keys, values)
    got, intra = lax.optimization_barrier((got, intra))
    entering = call(
        "scan",
        functools.partial(scan_kernel, pairs),
        [here],
        here,
        jax.ShapeDtypeStruct((count, piece, width), f32),
        2 * heads * width * width,
        3 * MIB,
        0,
        8,
    )(got)
    incoming = lax.all_to_all(entering, AXES, 0, 0, tiled=True).reshape(heads * width, width)
    scaled, gated = call(
        "ready",
        functools.partial(ready_kernel, width, chunks),
        [here, there, there, here],
        [there, there],
        [moved, moved],
        40 * rows * feats,
        16 * MIB,
        2 * rows * feats,
        56,
        [*[held] * 4, *[sems] * 4],
    )(cumul, queries, out_gate, norm_gain.reshape(1, feats))
    incoming, scaled, gated = lax.optimization_barrier((incoming, scaled, gated))
    return call(
        "final",
        functools.partial(final_kernel, width, 128, chunks),
        [here, there, there, there],
        there,
        moved,
        4 * rows * feats * width,
        17 * MIB,
        rows * feats,
        52,
        [*[held] * 4, *[sems] * 4],
    )(incoming, scaled, intra, gated)


def solution(mesh):
    split = P(AXES, None)
    count = 1
    for axis in AXES:
        count *= mesh.shape[axis]
    return jax.shard_map(
        functools.partial(on_device, count),
        mesh=mesh,
        in_specs=(split, split, split, P(None, AXES), split, P()),
        out_specs=split,
        check_vma=False,
    )
```

time: 77.3 us -> 69.8 us (0.903)
  Pallas kernels: 44.6 us -> 38.8 us
  local copies, waits for them, and re-layouts: 1.04 us -> 0 us
    pallas_call x5, Pallas kernels: 44.6 us -> 38.8 us  [the longest x1 13.7 us: on_device(): call('intra', functools.partial(intra_kernel, width, tile, chunks), [here...]
    all_to_all x1, waiting for transfers between devices: 7.57 us -> 5.22 us  [on_device(): got = lax.all_to_all(send, AXES, 0, 0, tiled=True)]
    all_to_all x1, waiting for transfers between devices: 5.93 us -> 7.86 us  [on_device(): lax.all_to_all(entering, AXES, 0, 0, tiled=True)]
    unnamed x2 -> x0, local copies, waits for them, and re-layouts: 1.04 us -> none
  transfers between devices with their start and end apart: 2 -> 2, of which waited for: 2 -> 2; matrix products, arithmetic and copies ran while one was open for 0% -> 0% of each run, Pallas kernels for 35% -> 34%
where the time goes in v2:
time: 69.8 us; the launch traced here: 69.5 us
  Pallas kernels  38.8 us (56%)
  starting transfers between devices  17.4 us (25%)
  waiting for transfers between devices  13.1 us (19%)
    pallas_call x1, Pallas kernels, on_device(): call('intra', functools.partial(intra_kernel, width, tile, chunks), [here...  13.7 us
    all_to_all x1, starting transfers between devices, on_device(): got = lax.all_to_all(send, AXES, 0, 0, tiled=True)  11.5 us
    pallas_call x1, Pallas kernels, on_device(): call('ready', functools.partial(ready_kernel, width, chunks), [here, ther...  9.77 us
    all_to_all x1, waiting for transfers between devices, on_device(): lax.all_to_all(entering, AXES, 0, 0, tiled=True)  7.86 us
    pallas_call x1, Pallas kernels, on_device(): call('final', functools.partial(final_kernel, width, 128, chunks), [here,...  7.36 us
    pallas_call x1, Pallas kernels, on_device(): call('states', functools.partial(state_kernel, width, piece, tile, chunks...  6.58 us
    all_to_all x1, starting transfers between devices, on_device(): lax.all_to_all(entering, AXES, 0, 0, tiled=True)  5.86 us
    all_to_all x1, waiting for transfers between devices, on_device(): got = lax.all_to_all(send, AXES, 0, 0, tiled=True)  5.22 us
  transfers between devices with their start and end apart: 2, of which 2 were waited for; matrix products, arithmetic and copies ran while one was open for 0% of the time, Pallas kernels for 34%

profile of v2, /device:TPU:1, one launch (start us, length us, event | category | flops | bytes accessed | tf_op | source)
XLA Modules:
  0.0 69.5 jit_solution(16579392760223506739)
XLA Ops:
  0.0 6.6 %states.1 = (f32[1152,2,128]{2,1,0:T(2,128)}, bf16[6144,128]{1,0:T(8,128)(2,1)}, f32[16,1024]{1,0:T(8,128)}) custom-call(f32[16,1024]{1,0:T(8,128)} %decay_ref.1, bf16[1024,2048]{1,0:T(8,128)(2,1)} %k_far.3, bf16[1024,2048]{1,0:T(8,128)(2,1)} %v_far.3), custom_call_target="tpu_custom_call" | custom-call | flops 536870912 | bytes 12582912 | tf_op jit(solution)/shard_map/states/pallas_call | solution.py:306
  6.6 11.5 %all-to-all-start = ((f32[1152,2,128]{2,1,0:T(2,128)}), f32[1152,2,128]{2,1,0:T(2,128)S(1)}, u32[]{:S(2)}, u32[]{:S(2)}) async-start(f32[1152,2,128]{2,1,0:T(2,128)} %get-tuple-element.15), calls=%async_computation | async-start | bytes 2359296 | tf_op jit(solution)/shard_map/all_to_all | solution.py:330
  18.1 13.7 %intra.1.intra_far = bf16[1024,2048]{1,0:T(8,128)(2,1)} custom-call(f32[16,1024]{1,0:T(8,128)} %get-tuple-element.16.cumul_ref, bf16[6144,128]{1,0:T(8,128)(2,1)} %get-tuple-element.17.near_ref, bf16[1024,2048]{1,0:T(8,128)(2,1)} %q_far.3, bf16[1024,2048]{1,0:T(8,128)(2,1)} %k_far.3, bf16[1024,2048]{1,0:T(8,128)(2,1)} %v_far.3), custom_call_target="tpu_custom_call" | custom-call | flops 2147483648 | bytes 18874368 | tf_op jit(solution)/shard_map/intra/pallas_call | solution.py:331
  31.8 5.2 %all-to-all-done.got_ref = f32[1152,2,128]{2,1,0:T(2,128)S(1)} async-done(((f32[1152,2,128]{2,1,0:T(2,128)}), f32[1152,2,128]{2,1,0:T(2,128)S(1)}, u32[]{:S(2)}, u32[]{:S(2)}) %all-to-all-start) | async-done | bytes 1179680 | tf_op jit(solution)/shard_map/all_to_all | solution.py:330
  37.0 1.4 %scan.1 = f32[128,16,128]{2,1,0:T(8,128)} custom-call(f32[1152,2,128]{2,1,0:T(2,128)S(1)} %all-to-all-done.got_ref), custom_call_target="tpu_custom_call" | custom-call | flops 524288 | bytes 3145728 | tf_op jit(solution)/shard_map/scan/pallas_call | solution.py:344
  38.4 5.9 %all-to-all-start.1 = ((f32[128,16,128]{2,1,0:T(8,128)}), f32[128,16,128]{2,1,0:T(8,128)S(1)}, u32[]{:S(2)}, u32[]{:S(2)}) async-start(f32[128,16,128]{2,1,0:T(8,128)} %scan.1), calls=%async_computation.1 | async-start | bytes 2097152 | tf_op jit(solution)/shard_map/all_to_all | solution.py:355
  44.3 9.8 %ready.1 = (bf16[1024,2048]{1,0:T(8,128)(2,1)}, bf16[1024,2048]{1,0:T(8,128)(2,1)}) custom-call(f32[16,1024]{1,0:T(8,128)} %get-tuple-element.16.cumul_ref, bf16[1024,2048]{1,0:T(8,128)(2,1)} %q_far.3, bf16[1024,2048]{1,0:T(8,128)(2,1)} %gate_far.1, f32[1,2048]{1,0:T(1,128)} %bitcast.3), custom_call_target="tpu_custom_call" | custom-call | flops 83886080 | bytes 16777216 | tf_op jit(solution)/shard_map/ready/pallas_call | solution.py:356
  54.1 7.9 %all-to-all-done.1 = f32[128,16,128]{2,1,0:T(8,128)S(1)} async-done(((f32[128,16,128]{2,1,0:T(8,128)}), f32[128,16,128]{2,1,0:T(8,128)S(1)}, u32[]{:S(2)}, u32[]{:S(2)}) %all-to-all-start.1) | async-done | bytes 1048608 | tf_op jit(solution)/shard_map/all_to_all | solution.py:355
  61.9 7.4 %final.1 = bf16[1024,2048]{1,0:T(8,128)(2,1)} custom-call(f32[2048,128]{1,0:T(8,128)S(1)} %bitcast.2, bf16[1024,2048]{1,0:T(8,128)(2,1)} %get-tuple-element.22.q_far, bf16[1024,2048]{1,0:T(8,128)(2,1)} %intra.1.intra_far, bf16[1024,2048]{1,0:T(8,128)(2,1)} %get-tuple-element.24.gated_far), custom_call_target="tpu_custom_call" | custom-call | flops 1073741824 | bytes 17825792 | tf_op jit(solution)/shard_map/final/pallas_call | solution.py:369
Async XLA Ops:
  6.6 30.4 %all-to-all-start = ((f32[1152,2,128]{2,1,0:T(2,128)}), f32[1152,2,128]{2,1,0:T(2,128)S(1)}, u32[]{:S(2)}, u32[]{:S(2)}) async-start(f32[1152,2,128]{2,1,0:T(2,128)} %get-tuple-element.15), calls=%async_computation | async-start | bytes 2359296 | tf_op jit(solution)/shard_map/all_to_all | solution.py:330
  38.4 23.5 %all-to-all-start.1 = ((f32[128,16,128]{2,1,0:T(8,128)}), f32[128,16,128]{2,1,0:T(8,128)S(1)}, u32[]{:S(2)}, u32[]{:S(2)}) async-start(f32[128,16,128]{2,1,0:T(8,128)} %scan.1), calls=%async_computation.1 | async-start | bytes 2097152 | tf_op jit(solution)/shard_map/all_to_all | solution.py:355

commit v3 on v2

--- a/solution.py
+++ b/solution.py
@@ -17,16 +17,17 @@
     a = lax.broadcasted_iota(jnp.int32, (128, 128), 0)
     b = lax.broadcasted_iota(jnp.int32, (128, 128), 1)
     upper = (a <= b).astype(jnp.float32)
+    pieces = [decay[:, c * 128 : (c + 1) * 128] for c in range(rows // 128)]
+    sums = jnp.dot(
+        jnp.concatenate(pieces, axis=0),
+        upper,
+        precision=lax.Precision.HIGHEST,
+        preferred_element_type=jnp.float32,
+    )
     carry = jnp.zeros((heads, 1), jnp.float32)
     parts = []
     for c in range(rows // 128):
-        part = jnp.dot(
-            decay[:, c * 128 : (c + 1) * 128],
-            upper,
-            precision=lax.Precision.HIGHEST,
-            preferred_element_type=jnp.float32,
-        )
-        part = part + carry
+        part = sums[c * heads : (c + 1) * heads] + carry
         carry = part[:, 127:128]
         parts.append(part)
     return jnp.concatenate(parts, axis=1)
@@ -113,7 +114,7 @@
         copy.wait()
 
 
-def scan_kernel(pairs, got_ref, out_ref):
+def scan_kernel(pairs, chunks, got_ref, out_far, out_ref, sems):
     count = out_ref.shape[0]
     width = got_ref.shape[2]
 
@@ -124,8 +125,17 @@
             out_ref[j, 2 * r : 2 * r + 2, :] = carry[r]
         return tuple(carry[r] * factor + got_ref[at + r] for r in range(pairs - 1))
 
-    zero = jnp.zeros((2, width), jnp.float32)
-    lax.fori_loop(0, count, lap, (zero,) * (pairs - 1), unroll=8)
+    carry = (jnp.zeros((2, width), jnp.float32),) * (pairs - 1)
+    each = count // chunks
+    sent = []
+    for c in range(chunks):
+        carry = lax.fori_loop(c * each, (c + 1) * each, lap, carry, unroll=8)
+        some = pl.ds(c * each, each)
+        copy = pltpu.make_async_copy(out_ref.at[some], out_far.at[some], sems.at[c])
+        copy.start()
+        sent.append(copy)
+    for copy in sent:
+        copy.wait()
 
 
 def intra_kernel(
@@ -279,12 +289,13 @@
     piece = heads * width // count
     tile = 256
     parts = rows // tile
-    chunks = 8
+    chunks, few = 8, 4
     f32, bf16 = jnp.float32, jnp.bfloat16
     here = pl.BlockSpec(memory_space=pltpu.VMEM)
     there = pl.BlockSpec(memory_space=pl.ANY)
     block = (rows, feats)
     sems = pltpu.SemaphoreType.DMA((chunks,))
+    few_sems = pltpu.SemaphoreType.DMA((few,))
     held = pltpu.VMEM(block, bf16)
     moved = jax.ShapeDtypeStruct(block, bf16)
 
@@ -305,7 +316,7 @@
     inner = (heads * (parts - 1) * width, width)
     send, near, cumul = call(
         "states",
-        functools.partial(state_kernel, width, piece, tile, chunks),
+        functools.partial(state_kernel, width, piece, tile, few),
         [here, there, there],
         [there, there, there],
         [
@@ -323,14 +334,14 @@
             pltpu.VMEM(message, f32),
             pltpu.VMEM(inner, bf16),
             pltpu.VMEM((heads, rows), f32),
-            *[sems] * 4,
+            *[few_sems] * 4,
             pltpu.SemaphoreType.DMA,
         ],
     )(log_decay, keys, values)
     got = lax.all_to_all(send, AXES, 0, 0, tiled=True)
     intra = call(
         "intra",
-        functools.partial(intra_kernel, width, tile, chunks),
+        functools.partial(intra_kernel, width, tile, few),
         [here, here, there, there, there],
         there,
         moved,
@@ -338,19 +349,20 @@
         18 * MIB,
         heads * rows * tile,
         56,
-        [*[held] * 4, *[sems] * 4],
+        [*[held] * 4, *[few_sems] * 4],
     )(cumul, near, queries, keys, values)
     got, intra = lax.optimization_barrier((got, intra))
     entering = call(
         "scan",
-        functools.partial(scan_kernel, pairs),
+        functools.partial(scan_kernel, pairs, few),
         [here],
-        here,
+        there,
         jax.ShapeDtypeStruct((count, piece, width), f32),
         2 * heads * width * width,
         3 * MIB,
         0,
         8,
+        [pltpu.VMEM((count, piece, width), f32), few_sems],
     )(got)
     incoming = lax.all_to_all(entering, AXES, 0, 0, tiled=True).reshape(heads * width, width)
     scaled, gated = call(

time: 69.8 us -> 69.3 us (level)
  Pallas kernels: 38.8 us -> 37.7 us
    pallas_call x3, Pallas kernels: 21.7 us -> 20.5 us  [the longest x1 13.1 us: on_device(): call('intra', functools.partial(intra_kernel, width, tile, few), [here, h...]
  transfers between devices with their start and end apart: 2 -> 2, of which waited for: 2 -> 2; matrix products, arithmetic and copies ran while one was open for 0% -> 0% of each run, Pallas kernels for 34% -> 33%
where the time goes in v3:
time: 69.3 us; the launch traced here: 68.9 us
  Pallas kernels  37.7 us (54%)
  starting transfers between devices  17.4 us (25%)
  waiting for transfers between devices  13.6 us (20%)
    pallas_call x1, Pallas kernels, on_device(): call('intra', functools.partial(intra_kernel, width, tile, few), [here, h...  13.1 us
    all_to_all x1, starting transfers between devices, on_device(): got = lax.all_to_all(send, AXES, 0, 0, tiled=True)  11.5 us
    pallas_call x1, Pallas kernels, on_device(): call('ready', functools.partial(ready_kernel, width, chunks), [here, ther...  9.77 us
    all_to_all x1, waiting for transfers between devices, on_device(): lax.all_to_all(entering, AXES, 0, 0, tiled=True)  7.86 us
    pallas_call x1, Pallas kernels, on_device(): call('final', functools.partial(final_kernel, width, 128, chunks), [here,...  7.36 us
    pallas_call x1, Pallas kernels, on_device(): call('states', functools.partial(state_kernel, width, piece, tile, few),...  6.23 us
    all_to_all x1, starting transfers between devices, on_device(): lax.all_to_all(entering, AXES, 0, 0, tiled=True)  5.87 us
    all_to_all x1, waiting for transfers between devices, on_device(): got = lax.all_to_all(send, AXES, 0, 0, tiled=True)  5.77 us
  transfers between devices with their start and end apart: 2, of which 2 were waited for; matrix products, arithmetic and copies ran while one was open for 0% of the time, Pallas kernels for 33%

profile of v3, /device:TPU:1, one launch (start us, length us, event | category | flops | bytes accessed | tf_op | source)
XLA Modules:
  0.0 68.9 jit_solution(14829228439450374010)
XLA Ops:
  0.0 6.2 %states.1 = (f32[1152,2,128]{2,1,0:T(2,128)}, bf16[6144,128]{1,0:T(8,128)(2,1)}, f32[16,1024]{1,0:T(8,128)}) custom-call(f32[16,1024]{1,0:T(8,128)} %decay_ref.1, bf16[1024,2048]{1,0:T(8,128)(2,1)} %k_far.3, bf16[1024,2048]{1,0:T(8,128)(2,1)} %v_far.3), custom_call_target="tpu_custom_call" | custom-call | flops 536870912 | bytes 12582912 | tf_op jit(solution)/shard_map/states/pallas_call | solution.py:317
  6.2 11.5 %all-to-all-start = ((f32[1152,2,128]{2,1,0:T(2,128)}), f32[1152,2,128]{2,1,0:T(2,128)S(1)}, u32[]{:S(2)}, u32[]{:S(2)}) async-start(f32[1152,2,128]{2,1,0:T(2,128)} %get-tuple-element.15), calls=%async_computation | async-start | bytes 2359296 | tf_op jit(solution)/shard_map/all_to_all | solution.py:341
  17.8 13.1 %intra.1.intra_far = bf16[1024,2048]{1,0:T(8,128)(2,1)} custom-call(f32[16,1024]{1,0:T(8,128)} %get-tuple-element.16.cumul_ref, bf16[6144,128]{1,0:T(8,128)(2,1)} %get-tuple-element.17.near_ref, bf16[1024,2048]{1,0:T(8,128)(2,1)} %q_far.3, bf16[1024,2048]{1,0:T(8,128)(2,1)} %k_far.3, bf16[1024,2048]{1,0:T(8,128)(2,1)} %v_far.3), custom_call_target="tpu_custom_call" | custom-call | flops 2147483648 | bytes 18874368 | tf_op jit(solution)/shard_map/intra/pallas_call | solution.py:342
  30.9 5.8 %all-to-all-done.got_ref = f32[1152,2,128]{2,1,0:T(2,128)S(1)} async-done(((f32[1152,2,128]{2,1,0:T(2,128)}), f32[1152,2,128]{2,1,0:T(2,128)S(1)}, u32[]{:S(2)}, u32[]{:S(2)}) %all-to-all-start) | async-done | bytes 1179680 | tf_op jit(solution)/shard_map/all_to_all | solution.py:341
  36.7 1.2 %scan.1 = f32[128,16,128]{2,1,0:T(8,128)} custom-call(f32[1152,2,128]{2,1,0:T(2,128)S(1)} %all-to-all-done.got_ref), custom_call_target="tpu_custom_call" | custom-call | flops 524288 | bytes 3145728 | tf_op jit(solution)/shard_map/scan/pallas_call | solution.py:355
  37.8 5.9 %all-to-all-start.1 = ((f32[128,16,128]{2,1,0:T(8,128)}), f32[128,16,128]{2,1,0:T(8,128)S(1)}, u32[]{:S(2)}, u32[]{:S(2)}) async-start(f32[128,16,128]{2,1,0:T(8,128)} %scan.1), calls=%async_computation.1 | async-start | bytes 2097152 | tf_op jit(solution)/shard_map/all_to_all | solution.py:367
  43.7 9.8 %ready.1 = (bf16[1024,2048]{1,0:T(8,128)(2,1)}, bf16[1024,2048]{1,0:T(8,128)(2,1)}) custom-call(f32[16,1024]{1,0:T(8,128)} %get-tuple-element.16.cumul_ref, bf16[1024,2048]{1,0:T(8,128)(2,1)} %q_far.3, bf16[1024,2048]{1,0:T(8,128)(2,1)} %gate_far.1, f32[1,2048]{1,0:T(1,128)} %bitcast.3), custom_call_target="tpu_custom_call" | custom-call | flops 83886080 | bytes 16777216 | tf_op jit(solution)/shard_map/ready/pallas_call | solution.py:368
  53.5 7.9 %all-to-all-done.1 = f32[128,16,128]{2,1,0:T(8,128)S(1)} async-done(((f32[128,16,128]{2,1,0:T(8,128)}), f32[128,16,128]{2,1,0:T(8,128)S(1)}, u32[]{:S(2)}, u32[]{:S(2)}) %all-to-all-start.1) | async-done | bytes 1048608 | tf_op jit(solution)/shard_map/all_to_all | solution.py:367
  61.4 7.4 %final.1 = bf16[1024,2048]{1,0:T(8,128)(2,1)} custom-call(f32[2048,128]{1,0:T(8,128)S(1)} %bitcast.2, bf16[1024,2048]{1,0:T(8,128)(2,1)} %get-tuple-element.22.q_far, bf16[1024,2048]{1,0:T(8,128)(2,1)} %intra.1.intra_far, bf16[1024,2048]{1,0:T(8,128)(2,1)} %get-tuple-element.24.gated_far), custom_call_target="tpu_custom_call" | custom-call | flops 1073741824 | bytes 17825792 | tf_op jit(solution)/shard_map/final/pallas_call | solution.py:381
Async XLA Ops:
  6.2 30.4 %all-to-all-start = ((f32[1152,2,128]{2,1,0:T(2,128)}), f32[1152,2,128]{2,1,0:T(2,128)S(1)}, u32[]{:S(2)}, u32[]{:S(2)}) async-start(f32[1152,2,128]{2,1,0:T(2,128)} %get-tuple-element.15), calls=%async_computation | async-start | bytes 2359296 | tf_op jit(solution)/shard_map/all_to_all | solution.py:341
  37.8 23.5 %all-to-all-start.1 = ((f32[128,16,128]{2,1,0:T(8,128)}), f32[128,16,128]{2,1,0:T(8,128)S(1)}, u32[]{:S(2)}, u32[]{:S(2)}) async-start(f32[128,16,128]{2,1,0:T(8,128)} %scan.1), calls=%async_computation.1 | async-start | bytes 2097152 | tf_op jit(solution)/shard_map/all_to_all | solution.py:367

commit v4 on v3

--- a/solution.py
+++ b/solution.py
@@ -40,14 +40,21 @@
     )
 
 
-def fetch(source, target, sems, chunks):
-    wide = source.shape[1] // chunks
+def fetch(source, target, sems, heads, width):
+    edges = borders(heads)
     return [
         pltpu.make_async_copy(
-            source.at[:, pl.ds(c * wide, wide)], target.at[:, pl.ds(c * wide, wide)], sems.at[c]
+            source.at[:, pl.ds(first * width, (last - first) * width)],
+            target.at[:, pl.ds(first * width, (last - first) * width)],
+            sems.at[c],
         )
-        for c in range(chunks)
+        for c, (first, last) in enumerate(zip(edges, edges[1:]))
     ]
+
+
+def borders(heads):
+    small, large = heads // 8, heads // 4
+    return [0, *(small + n * large for n in range(4)), heads]
 
 
 def state_kernel(
@@ -56,9 +63,8 @@
 ):
     rows, feats = k_ref.shape
     heads = feats // width
-    copies = list(zip(fetch(k_far, k_ref, k_sems, chunks), fetch(v_far, v_ref, v_sems, chunks)))
-    ahead = 4
-    for pair in copies[:ahead]:
+    copies = list(zip(fetch(k_far, k_ref, k_sems, heads, width), fetch(v_far, v_ref, v_sems, heads, width)))
+    for pair in copies:
         for copy in pair:
             copy.start()
     cumul = running_sum(decay_ref[...])
@@ -66,18 +72,15 @@
     cumul_copy = pltpu.make_async_copy(cumul_ref, cumul_far, cumul_sem)
     cumul_copy.start()
 
-    group = heads // chunks
+    edges = borders(heads)
     per = width // piece
     pairs = piece // 2 + 1
     parts = rows // tile
     sent = []
-    for c in range(chunks):
+    for c, (first, last) in enumerate(zip(edges, edges[1:])):
         for copy in copies[c]:
             copy.wait()
-        if c + ahead < chunks:
-            for copy in copies[c + ahead]:
-                copy.start()
-        for i in range(c * group, (c + 1) * group):
+        for i in range(first, last):
             row = cumul[i : i + 1, :]
             cut = slice(i * width, (i + 1) * width)
             before = jnp.zeros((1, 1), jnp.float32)
@@ -102,10 +105,10 @@
                     stage_ref[at + r, :, :] = state[from_row : from_row + 2, :]
                 stage_ref[at + pairs - 1, :, :] = factor
         for held, far, sem, each in (
-            (stage_ref, send_far, sems, group * per * pairs),
-            (near_ref, near_far, near_sems, group * (parts - 1) * width),
+            (stage_ref, send_far, sems, per * pairs),
+            (near_ref, near_far, near_sems, (parts - 1) * width),
         ):
-            some = pl.ds(c * each, each)
+            some = pl.ds(first * each, (last - first) * each)
             copy = pltpu.make_async_copy(held.at[some], far.at[some], sem.at[c])
             copy.start()
             sent.append(copy)
@@ -144,15 +147,15 @@
 ):
     rows, feats = q_ref.shape
     heads = feats // width
-    group = heads // chunks
+    edges = borders(heads)
     copies = list(
         zip(
-            fetch(q_far, q_ref, q_sems, chunks),
-            fetch(k_far, k_ref, k_sems, chunks),
-            fetch(v_far, v_ref, v_sems, chunks),
+            fetch(q_far, q_ref, q_sems, heads, width),
+            fetch(k_far, k_ref, k_sems, heads, width),
+            fetch(v_far, v_ref, v_sems, heads, width),
         )
     )
-    sent = fetch(out_ref, out_far, sems, chunks)
+    sent = fetch(out_ref, out_far, sems, heads, width)
     for some in copies:
         for copy in some:
             copy.start()
@@ -164,8 +167,8 @@
         [cumul_ref[...], jnp.zeros((width - heads, rows), jnp.float32)], axis=0
     ).T
     for i in range(0, heads, 2):
-        if i % group == 0:
-            for copy in copies[i // group]:
+        if i in edges:
+            for copy in copies[edges.index(i)]:
                 copy.wait()
         row = [cumul_ref[i + n : i + n + 1, :] for n in range(2)]
         col = [columns[:, i + n : i + n + 1] for n in range(2)]
@@ -195,8 +198,8 @@
                     edge = row[n][:, start - 1 : start]
                     intra = intra + jnp.exp(col[n][mine] - edge) * far[:, n * width : (n + 1) * width]
                 out_ref[mine, cut] = intra.astype(out_ref.dtype)
-        if (i + 2) % group == 0:
-            sent[i // group].start()
+        if i + 2 in edges:
+            sent[edges.index(i + 2) - 1].start()
     for copy in sent:
         copy.wait()
 
@@ -207,32 +210,32 @@
 ):
     rows, feats = q_ref.shape
     heads = feats // width
-    gates = fetch(gate_far, gate_ref, gate_sems, chunks)
-    queries = fetch(q_far, q_ref, q_sems, chunks)
+    gates = fetch(gate_far, gate_ref, gate_sems, heads, width)
+    queries = fetch(q_far, q_ref, q_sems, heads, width)
     sent = list(
         zip(
-            fetch(scaled_ref, scaled_far, scaled_sems, chunks),
-            fetch(gated_ref, gated_far, gated_sems, chunks),
+            fetch(scaled_ref, scaled_far, scaled_sems, heads, width),
+            fetch(gated_ref, gated_far, gated_sems, heads, width),
         )
     )
-    group = heads // chunks
-    for c in range(chunks):
-        gates[c].start()
-        queries[c].start()
+    edges = borders(heads)
+    for pair in zip(gates, queries):
+        for copy in pair:
+            copy.start()
     columns = jnp.concatenate(
         [jnp.exp(cumul_ref[...]), jnp.zeros((width - heads, rows), jnp.float32)], axis=0
     ).T
     for i in range(heads):
-        if i % group == 0:
-            gates[i // group].wait()
-            queries[i // group].wait()
+        if i in edges:
+            gates[edges.index(i)].wait()
+            queries[edges.index(i)].wait()
         cut = slice(i * width, (i + 1) * width)
         half = gate_ref[:, cut].astype(jnp.float32) * 0.5
         gated_ref[:, cut] = (gain_ref[:, cut] * (half + half * jnp.tanh(half))).astype(gated_ref.dtype)
         scaled = q_ref[:, cut].astype(jnp.float32) * columns[:, i : i + 1]
         scaled_ref[:, cut] = scaled.astype(scaled_ref.dtype)
-        if (i + 1) % group == 0:
-            for copy in sent[i // group]:
+        if i + 1 in edges:
+            for copy in sent[edges.index(i + 1) - 1]:
                 copy.start()
     for some in sent:
         for copy in some:
@@ -245,23 +248,23 @@
 ):
     rows, feats = q_ref.shape
     heads = feats // width
-    group = heads // chunks
+    edges = borders(heads)
     copies = list(
         zip(
-            fetch(q_far, q_ref, q_sems, chunks),
-            fetch(intra_far, intra_ref, intra_sems, chunks),
-            fetch(gated_far, gated_ref, gated_sems, chunks),
+            fetch(q_far, q_ref, q_sems, heads, width),
+            fetch(intra_far, intra_ref, intra_sems, heads, width),
+            fetch(gated_far, gated_ref, gated_sems, heads, width),
         )
     )
-    sent = fetch(out_ref, out_far, sems, chunks)
+    sent = fetch(out_ref, out_far, sems, heads, width)
     for some in copies:
         for copy in some:
             copy.start()
     share = jnp.full((width, width), 1.0 / width, jnp.bfloat16)
     share = across(share, share)
     for i in range(0, heads, 2):
-        if i % group == 0:
-            for copy in copies[i // group]:
+        if i in edges:
+            for copy in copies[edges.index(i)]:
                 copy.wait()
         both = slice(i * width, (i + 2) * width)
         state = state_ref[i * width : (i + 2) * width, :].astype(jnp.bfloat16)
@@ -276,8 +279,8 @@
             )
             out = mixed * lax.rsqrt(power + 1e-6) * gated_ref[mine, both].astype(jnp.float32)
             out_ref[mine, both] = out.astype(jnp.bfloat16)
-        if (i + 2) % group == 0:
-            sent[i // group].start()
+        if i + 2 in edges:
+            sent[edges.index(i + 2) - 1].start()
     for copy in sent:
         copy.wait()
 
@@ -294,7 +297,7 @@
     here = pl.BlockSpec(memory_space=pltpu.VMEM)
     there = pl.BlockSpec(memory_space=pl.ANY)
     block = (rows, feats)
-    sems = pltpu.SemaphoreType.DMA((chunks,))
+    sems = pltpu.SemaphoreType.DMA((len(borders(heads)) - 1,))
     few_sems = pltpu.SemaphoreType.DMA((few,))
     held = pltpu.VMEM(block, bf16)
     moved = jax.ShapeDtypeStruct(block, bf16)
@@ -334,7 +337,7 @@
             pltpu.VMEM(message, f32),
             pltpu.VMEM(inner, bf16),
             pltpu.VMEM((heads, rows), f32),
-            *[few_sems] * 4,
+            *[sems] * 4,
             pltpu.SemaphoreType.DMA,
         ],
     )(log_decay, keys, values)
@@ -349,7 +352,7 @@
         18 * MIB,
         heads * rows * tile,
         56,
-        [*[held] * 4, *[few_sems] * 4],
+        [*[held] * 4, *[sems] * 4],
     )(cumul, near, queries, keys, values)
     got, intra = lax.optimization_barrier((got, intra))
     entering = call(

time: 69.3 us -> 69.1 us (level)
  Pallas kernels: 37.7 us -> 36.8 us
  waiting for transfers between devices: 13.6 us -> 14.4 us
  transfers between devices with their start and end apart: 2 -> 2, of which waited for: 2 -> 2; matrix products, arithmetic and copies ran while one was open for 0% -> 0% of each run, Pallas kernels for 33% -> 32%
where the time goes in v4:
time: 69.1 us; the launch traced here: 68.8 us
  Pallas kernels  36.8 us (53%)
  starting transfers between devices  17.4 us (25%)
  waiting for transfers between devices  14.4 us (21%)
    pallas_call x1, Pallas kernels, on_device(): call('intra', functools.partial(intra_kernel, width, tile, few), [here, h...  12.7 us
    all_to_all x1, starting transfers between devices, on_device(): got = lax.all_to_all(send, AXES, 0, 0, tiled=True)  11.5 us
    pallas_call x1, Pallas kernels, on_device(): call('ready', functools.partial(ready_kernel, width, chunks), [here, ther...  9.44 us
    all_to_all x1, waiting for transfers between devices, on_device(): lax.all_to_all(entering, AXES, 0, 0, tiled=True)  8.2 us
    pallas_call x1, Pallas kernels, on_device(): call('final', functools.partial(final_kernel, width, 128, chunks), [here,...  7.28 us
    pallas_call x1, Pallas kernels, on_device(): call('states', functools.partial(state_kernel, width, piece, tile, few),...  6.16 us
    all_to_all x1, waiting for transfers between devices, on_device(): got = lax.all_to_all(send, AXES, 0, 0, tiled=True)  6.15 us
    all_to_all x1, starting transfers between devices, on_device(): lax.all_to_all(entering, AXES, 0, 0, tiled=True)  5.87 us
  transfers between devices with their start and end apart: 2, of which 2 were waited for; matrix products, arithmetic and copies ran while one was open for 0% of the time, Pallas kernels for 32%

profile of v4, /device:TPU:1, one launch (start us, length us, event | category | flops | bytes accessed | tf_op | source)
XLA Modules:
  0.0 68.8 jit_solution(8759972755259135737)
XLA Ops:
  0.0 6.2 %states.1 = (f32[1152,2,128]{2,1,0:T(2,128)}, bf16[6144,128]{1,0:T(8,128)(2,1)}, f32[16,1024]{1,0:T(8,128)}) custom-call(f32[16,1024]{1,0:T(8,128)} %decay_ref.1, bf16[1024,2048]{1,0:T(8,128)(2,1)} %k_far.3, bf16[1024,2048]{1,0:T(8,128)(2,1)} %v_far.3), custom_call_target="tpu_custom_call" | custom-call | flops 536870912 | bytes 12582912 | tf_op jit(solution)/shard_map/states/pallas_call | solution.py:320
  6.2 11.5 %all-to-all-start = ((f32[1152,2,128]{2,1,0:T(2,128)}), f32[1152,2,128]{2,1,0:T(2,128)S(1)}, u32[]{:S(2)}, u32[]{:S(2)}) async-start(f32[1152,2,128]{2,1,0:T(2,128)} %get-tuple-element.15), calls=%async_computation | async-start | bytes 2359296 | tf_op jit(solution)/shard_map/all_to_all | solution.py:344
  17.7 12.7 %intra.1.intra_far = bf16[1024,2048]{1,0:T(8,128)(2,1)} custom-call(f32[16,1024]{1,0:T(8,128)} %get-tuple-element.16.cumul_ref, bf16[6144,128]{1,0:T(8,128)(2,1)} %get-tuple-element.17.near_ref, bf16[1024,2048]{1,0:T(8,128)(2,1)} %q_far.3, bf16[1024,2048]{1,0:T(8,128)(2,1)} %k_far.3, bf16[1024,2048]{1,0:T(8,128)(2,1)} %v_far.3), custom_call_target="tpu_custom_call" | custom-call | flops 2147483648 | bytes 18874368 | tf_op jit(solution)/shard_map/intra/pallas_call | solution.py:345
  30.4 6.2 %all-to-all-done.got_ref = f32[1152,2,128]{2,1,0:T(2,128)S(1)} async-done(((f32[1152,2,128]{2,1,0:T(2,128)}), f32[1152,2,128]{2,1,0:T(2,128)S(1)}, u32[]{:S(2)}, u32[]{:S(2)}) %all-to-all-start) | async-done | bytes 1179680 | tf_op jit(solution)/shard_map/all_to_all | solution.py:344
  36.6 1.2 %scan.1 = f32[128,16,128]{2,1,0:T(8,128)} custom-call(f32[1152,2,128]{2,1,0:T(2,128)S(1)} %all-to-all-done.got_ref), custom_call_target="tpu_custom_call" | custom-call | flops 524288 | bytes 3145728 | tf_op jit(solution)/shard_map/scan/pallas_call | solution.py:358
  37.8 5.9 %all-to-all-start.1 = ((f32[128,16,128]{2,1,0:T(8,128)}), f32[128,16,128]{2,1,0:T(8,128)S(1)}, u32[]{:S(2)}, u32[]{:S(2)}) async-start(f32[128,16,128]{2,1,0:T(8,128)} %scan.1), calls=%async_computation.1 | async-start | bytes 2097152 | tf_op jit(solution)/shard_map/all_to_all | solution.py:370
  43.6 9.4 %ready.1 = (bf16[1024,2048]{1,0:T(8,128)(2,1)}, bf16[1024,2048]{1,0:T(8,128)(2,1)}) custom-call(f32[16,1024]{1,0:T(8,128)} %get-tuple-element.16.cumul_ref, bf16[1024,2048]{1,0:T(8,128)(2,1)} %q_far.3, bf16[1024,2048]{1,0:T(8,128)(2,1)} %gate_far.1, f32[1,2048]{1,0:T(1,128)} %bitcast.3), custom_call_target="tpu_custom_call" | custom-call | flops 83886080 | bytes 16777216 | tf_op jit(solution)/shard_map/ready/pallas_call | solution.py:371
  53.1 8.2 %all-to-all-done.1 = f32[128,16,128]{2,1,0:T(8,128)S(1)} async-done(((f32[128,16,128]{2,1,0:T(8,128)}), f32[128,16,128]{2,1,0:T(8,128)S(1)}, u32[]{:S(2)}, u32[]{:S(2)}) %all-to-all-start.1) | async-done | bytes 1048608 | tf_op jit(solution)/shard_map/all_to_all | solution.py:370
  61.3 7.3 %final.1 = bf16[1024,2048]{1,0:T(8,128)(2,1)} custom-call(f32[2048,128]{1,0:T(8,128)S(1)} %bitcast.2, bf16[1024,2048]{1,0:T(8,128)(2,1)} %get-tuple-element.22.q_far, bf16[1024,2048]{1,0:T(8,128)(2,1)} %intra.1.intra_far, bf16[1024,2048]{1,0:T(8,128)(2,1)} %get-tuple-element.24.gated_far), custom_call_target="tpu_custom_call" | custom-call | flops 1073741824 | bytes 17825792 | tf_op jit(solution)/shard_map/final/pallas_call | solution.py:384
Async XLA Ops:
  6.2 30.4 %all-to-all-start = ((f32[1152,2,128]{2,1,0:T(2,128)}), f32[1152,2,128]{2,1,0:T(2,128)S(1)}, u32[]{:S(2)}, u32[]{:S(2)}) async-start(f32[1152,2,128]{2,1,0:T(2,128)} %get-tuple-element.15), calls=%async_computation | async-start | bytes 2359296 | tf_op jit(solution)/shard_map/all_to_all | solution.py:344
  37.8 23.5 %all-to-all-start.1 = ((f32[128,16,128]{2,1,0:T(8,128)}), f32[128,16,128]{2,1,0:T(8,128)S(1)}, u32[]{:S(2)}, u32[]{:S(2)}) async-start(f32[128,16,128]{2,1,0:T(8,128)} %scan.1), calls=%async_computation.1 | async-start | bytes 2097152 | tf_op jit(solution)/shard_map/all_to_all | solution.py:370
